TPU v7x, 256 devices: a whole 4x4x8 slice. The times are simulated.
256 devices in a mesh: ctx: 32 (over y, z), tp: 8 (over x, core).
Axes of the slice: x: 4, y: 4, z: 8, core: 2. Of those that a mesh axis runs over, the one named last changes fastest.
Arguments:
- queries: bfloat16 [12288, 8192], P('ctx', 'tp'), may hold values from -96 to 96
- keys: bfloat16 [12288, 1024], P('ctx', 'tp'), may hold values from -6 to 6
- values: bfloat16 [12288, 1024], P('ctx', 'tp'), may hold values from -6 to 6
- doc_lengths: int32 [24], replicated, may hold values from 1 to 6912, 12288 in all
- out_weight: bfloat16 [8192, 5120], P('tp'), may hold values from -0.0625 to 0.0625
Outputs:
- projected: bfloat16 [12288, 5120], P('ctx', 'tp')
Inputs may be any that keep to these rules, and one draw needn't show every extreme that they name: `doc_lengths`: positive lengths of the 24 documents in order; they sum to 12288 and the longest is exactly 6912.
All inputs are finite; a program needn't handle non-finite values.
Results may differ from a plain program's by a relative error of at most 0.017.
Values may be sent and summed in bfloat16 or wider, within the bound.
A program may use at most 64 MiB of HBM per device.

v0:
```python
import math

import jax
import jax.numpy as jnp
from jax import lax
from jax.sharding import PartitionSpec as P

HEAD_SIZE = 128


def doc_begin(doc_lengths, positions):
    doc_ends = jnp.cumsum(doc_lengths)
    doc_firsts = doc_ends - doc_lengths
    covered = doc_firsts[None, :] <= positions[:, None]
    return jnp.max(jnp.where(covered, doc_firsts[None, :], 0), axis=1)


def fresh_state(query_count, kv_count, group_length):
    shape_three = (query_count, kv_count, group_length)
    return (
        jnp.full(shape_three, -1e30, jnp.float32),
        jnp.zeros(shape_three, jnp.float32),
        jnp.zeros(shape_three + (HEAD_SIZE,), jnp.float32),
    )


def attend(carry_state, query_mat, query_pos, query_doc, key_vals, key_first):
    running_max, weight_total, accumulated = carry_state
    key_count = key_vals.shape[0]
    kv_count = query_mat.shape[1]
    key_mat = key_vals[:, : kv_count * HEAD_SIZE].reshape(key_count, kv_count, HEAD_SIZE)
    value_mat = key_vals[:, kv_count * HEAD_SIZE :].reshape(key_count, kv_count, HEAD_SIZE)
    key_pos = key_first + jnp.arange(key_count, dtype=jnp.int32)
    visible = (key_pos[None, :] >= query_doc[:, None]) & (key_pos[None, :] <= query_pos[:, None])
    visible = visible[:, None, None, :]
    scores = jnp.einsum(
        "rgjd,kgd->rgjk", query_mat, key_mat, preferred_element_type=jnp.float32
    ) * (1.0 / math.sqrt(HEAD_SIZE))
    new_max = jnp.maximum(running_max, jnp.max(jnp.where(visible, scores, -1e30), axis=-1))
    rescale = jnp.exp(running_max - new_max)
    weights = jnp.where(visible, jnp.exp(scores - new_max[..., None]), 0.0)
    weight_total = weight_total * rescale + jnp.sum(weights, axis=-1)
    accumulated = accumulated * rescale[..., None] + jnp.einsum(
        "rgjk,kgd->rgjd",
        weights.astype(jnp.bfloat16),
        value_mat,
        preferred_element_type=jnp.float32,
    )
    return (new_max, weight_total, accumulated)


def guarded(carry_state, query_mat, query_pos, query_doc, key_vals, key_first):
    key_count = key_vals.shape[0]
    needed = (key_first + key_count - 1 >= jnp.min(query_doc)) & (key_first <= jnp.max(query_pos))
    return lax.cond(
        needed,
        lambda inner: attend(inner, query_mat, query_pos, query_doc, key_vals, key_first),
        lambda inner: inner,
        carry_state,
    )


def sweep(carry_state, query_mat, query_pos, query_doc, key_vals, key_first):
    total_keys = key_vals.shape[0]
    key_block = 1
    for candidate in range(1, min(total_keys, 512) + 1):
        if total_keys % candidate == 0:
            key_block = candidate

    def visit(block_number, inner):
        piece_keys = lax.dynamic_slice_in_dim(key_vals, block_number * key_block, key_block, 0)
        return guarded(
            inner, query_mat, query_pos, query_doc, piece_keys, key_first + block_number * key_block
        )

    return lax.fori_loop(0, total_keys // key_block, visit, carry_state)


def finish(carry_state):
    running_max, weight_total, accumulated = carry_state
    normed = accumulated / weight_total[..., None]
    return normed.astype(jnp.bfloat16).reshape(accumulated.shape[0], -1)


def local(queries, keys, values, doc_lengths, out_weight):
    tok_rows = queries.shape[0]
    kv_count = keys.shape[1] // HEAD_SIZE
    group_length = queries.shape[1] // keys.shape[1]
    ctx_index = lax.axis_index("ctx")
    stacked = jnp.concatenate([keys, values], axis=1)
    own_pos = ctx_index * tok_rows + jnp.arange(tok_rows, dtype=jnp.int32)
    query_mat = queries.reshape(tok_rows, kv_count, group_length, HEAD_SIZE)
    query_doc = doc_begin(doc_lengths, own_pos)
    final_state = sweep(
        fresh_state(tok_rows, kv_count, group_length),
        query_mat,
        own_pos,
        query_doc,
        lax.all_gather(stacked, "ctx", axis=0, tiled=True),
        jnp.int32(0),
    )
    result_rows = finish(final_state)
    summed = lax.psum_scatter(
        lax.dot_general(
            out_weight, result_rows, (((0,), (1,)), ((), ())), preferred_element_type=jnp.float32
        ).astype(jnp.bfloat16),
        "tp",
        scatter_dimension=0,
        tiled=True,
    ).astype(jnp.float32)
    return summed.T.astype(jnp.bfloat16)


def solution(mesh):
    in_specs = (P("ctx", "tp"), P("ctx", "tp"), P("ctx", "tp"), P(), P("tp", None))
    out_specs = P("ctx", "tp")
    return jax.shard_map(local, mesh=mesh, in_specs=in_specs, out_specs=out_specs, check_vma=False)
```

profile of v0, /device:TPU:16, one launch (start us, length us, event | category | flops | bytes accessed | tf_op | source)
XLA Modules:
  0.0 283.5 jit_solution(11979135863099281221)
XLA Ops:
  13.1 86.8 %all-gather.2.cloned.1.call-done = bf16[12288,256]{1,0:T(8,128)(2,1)} async-done(((bf16[384,256]{1,0:T(8,128)(2,1)}), bf16[12288,256]{1,0:T(8,128)(2,1)}) %all-gather.2.cloned.1.call-update) | async-done | bytes 6291472 | tf_op jit(solution)/shard_map/all_gather | solution.py:99
  100.0 100.9 %while.22 = (s32[]{:T(128)}, f32[384,1,8]{0,2,1:T(8,128)S(1)}, f32[384,1,8]{0,2,1:T(8,128)S(1)}, f32[384,1,8,128]{0,3,2,1:T(8,128)S(1)}, s32[]{:T(128)}, /*index...) while((s32[]{:T(128)}, f32[384,1,8]{0,2,1:T(8,128)S(1)}, ...), condition=%wide.region_9.10_spmd.clone, body=%wide.region_4.9_spmd.clone.sunk | while | flops 823994240 | bytes 24063856 | solution.py:76
  104.0 6.3 %conditional.3 = ((f32[384,1,8]{0,2,1:T(8,128)S(1)}, f32[384,1,8]{0,2,1:T(8,128)S(1)}, f32[384,1,8,128]{0,3,2,1:T(8,128)S(1)})) conditional(s32[]{:T(128)} %convert_element_type.48, (f32[384,1,8]{0,2,1:T(8,128)S(1)}, f32[384,1,8]{0,2,1:T(8,128)S(1)}, f32[384,1,8,128]{0,3,2,1:T(8,128)S(1)}) %tuple.75, (s32[]{:T(128)}, s32[384]{0:T(512)S(1)}, ...), branch_computations={%region_5.5_spmd, %region_6.8_spmd} | conditional | flops 823994240 | bytes 24062050 | solution.py:55
  106.3 2.6 bitcast_add_fusion
  111.6 6.3 %conditional.3 = ((f32[384,1,8]{0,2,1:T(8,128)S(1)}, f32[384,1,8]{0,2,1:T(8,128)S(1)}, f32[384,1,8,128]{0,3,2,1:T(8,128)S(1)})) conditional(s32[]{:T(128)} %convert_element_type.48, (f32[384,1,8]{0,2,1:T(8,128)S(1)}, f32[384,1,8]{0,2,1:T(8,128)S(1)}, f32[384,1,8,128]{0,3,2,1:T(8,128)S(1)}) %tuple.75, (s32[]{:T(128)}, s32[384]{0:T(512)S(1)}, ...), branch_computations={%region_5.5_spmd, %region_6.8_spmd} | conditional | flops 823994240 | bytes 24062050 | solution.py:55
  113.9 2.6 bitcast_add_fusion
  119.2 6.3 %conditional.3 = ((f32[384,1,8]{0,2,1:T(8,128)S(1)}, f32[384,1,8]{0,2,1:T(8,128)S(1)}, f32[384,1,8,128]{0,3,2,1:T(8,128)S(1)})) conditional(s32[]{:T(128)} %convert_element_type.48, (f32[384,1,8]{0,2,1:T(8,128)S(1)}, f32[384,1,8]{0,2,1:T(8,128)S(1)}, f32[384,1,8,128]{0,3,2,1:T(8,128)S(1)}) %tuple.75, (s32[]{:T(128)}, s32[384]{0:T(512)S(1)}, ...), branch_computations={%region_5.5_spmd, %region_6.8_spmd} | conditional | flops 823994240 | bytes 24062050 | solution.py:55
  119.5 2.0 fusion.2
  121.5 2.6 bitcast_add_fusion
  126.8 6.3 %conditional.3 = ((f32[384,1,8]{0,2,1:T(8,128)S(1)}, f32[384,1,8]{0,2,1:T(8,128)S(1)}, f32[384,1,8,128]{0,3,2,1:T(8,128)S(1)})) conditional(s32[]{:T(128)} %convert_element_type.48, (f32[384,1,8]{0,2,1:T(8,128)S(1)}, f32[384,1,8]{0,2,1:T(8,128)S(1)}, f32[384,1,8,128]{0,3,2,1:T(8,128)S(1)}) %tuple.75, (s32[]{:T(128)}, s32[384]{0:T(512)S(1)}, ...), branch_computations={%region_5.5_spmd, %region_6.8_spmd} | conditional | flops 823994240 | bytes 24062050 | solution.py:55
  127.1 2.0 fusion.2
  129.2 2.6 bitcast_add_fusion
  134.4 6.3 %conditional.3 = ((f32[384,1,8]{0,2,1:T(8,128)S(1)}, f32[384,1,8]{0,2,1:T(8,128)S(1)}, f32[384,1,8,128]{0,3,2,1:T(8,128)S(1)})) conditional(s32[]{:T(128)} %convert_element_type.48, (f32[384,1,8]{0,2,1:T(8,128)S(1)}, f32[384,1,8]{0,2,1:T(8,128)S(1)}, f32[384,1,8,128]{0,3,2,1:T(8,128)S(1)}) %tuple.75, (s32[]{:T(128)}, s32[384]{0:T(512)S(1)}, ...), branch_computations={%region_5.5_spmd, %region_6.8_spmd} | conditional | flops 823994240 | bytes 24062050 | solution.py:55
  134.7 2.0 fusion.2
  136.8 2.6 bitcast_add_fusion
  142.0 6.3 %conditional.3 = ((f32[384,1,8]{0,2,1:T(8,128)S(1)}, f32[384,1,8]{0,2,1:T(8,128)S(1)}, f32[384,1,8,128]{0,3,2,1:T(8,128)S(1)})) conditional(s32[]{:T(128)} %convert_element_type.48, (f32[384,1,8]{0,2,1:T(8,128)S(1)}, f32[384,1,8]{0,2,1:T(8,128)S(1)}, f32[384,1,8,128]{0,3,2,1:T(8,128)S(1)}) %tuple.75, (s32[]{:T(128)}, s32[384]{0:T(512)S(1)}, ...), branch_computations={%region_5.5_spmd, %region_6.8_spmd} | conditional | flops 823994240 | bytes 24062050 | solution.py:55
  142.3 2.0 fusion.2
  144.4 2.6 bitcast_add_fusion
  149.7 6.3 %conditional.3 = ((f32[384,1,8]{0,2,1:T(8,128)S(1)}, f32[384,1,8]{0,2,1:T(8,128)S(1)}, f32[384,1,8,128]{0,3,2,1:T(8,128)S(1)})) conditional(s32[]{:T(128)} %convert_element_type.48, (f32[384,1,8]{0,2,1:T(8,128)S(1)}, f32[384,1,8]{0,2,1:T(8,128)S(1)}, f32[384,1,8,128]{0,3,2,1:T(8,128)S(1)}) %tuple.75, (s32[]{:T(128)}, s32[384]{0:T(512)S(1)}, ...), branch_computations={%region_5.5_spmd, %region_6.8_spmd} | conditional | flops 823994240 | bytes 24062050 | solution.py:55
  152.0 2.6 bitcast_add_fusion
  157.3 6.3 %conditional.3 = ((f32[384,1,8]{0,2,1:T(8,128)S(1)}, f32[384,1,8]{0,2,1:T(8,128)S(1)}, f32[384,1,8,128]{0,3,2,1:T(8,128)S(1)})) conditional(s32[]{:T(128)} %convert_element_type.48, (f32[384,1,8]{0,2,1:T(8,128)S(1)}, f32[384,1,8]{0,2,1:T(8,128)S(1)}, f32[384,1,8,128]{0,3,2,1:T(8,128)S(1)}) %tuple.75, (s32[]{:T(128)}, s32[384]{0:T(512)S(1)}, ...), branch_computations={%region_5.5_spmd, %region_6.8_spmd} | conditional | flops 823994240 | bytes 24062050 | solution.py:55
  157.5 2.0 fusion.2
  159.6 2.6 bitcast_add_fusion
  164.9 6.3 %conditional.3 = ((f32[384,1,8]{0,2,1:T(8,128)S(1)}, f32[384,1,8]{0,2,1:T(8,128)S(1)}, f32[384,1,8,128]{0,3,2,1:T(8,128)S(1)})) conditional(s32[]{:T(128)} %convert_element_type.48, (f32[384,1,8]{0,2,1:T(8,128)S(1)}, f32[384,1,8]{0,2,1:T(8,128)S(1)}, f32[384,1,8,128]{0,3,2,1:T(8,128)S(1)}) %tuple.75, (s32[]{:T(128)}, s32[384]{0:T(512)S(1)}, ...), branch_computations={%region_5.5_spmd, %region_6.8_spmd} | conditional | flops 823994240 | bytes 24062050 | solution.py:55
  167.2 2.6 bitcast_add_fusion
  172.5 6.3 %conditional.3 = ((f32[384,1,8]{0,2,1:T(8,128)S(1)}, f32[384,1,8]{0,2,1:T(8,128)S(1)}, f32[384,1,8,128]{0,3,2,1:T(8,128)S(1)})) conditional(s32[]{:T(128)} %convert_element_type.48, (f32[384,1,8]{0,2,1:T(8,128)S(1)}, f32[384,1,8]{0,2,1:T(8,128)S(1)}, f32[384,1,8,128]{0,3,2,1:T(8,128)S(1)}) %tuple.75, (s32[]{:T(128)}, s32[384]{0:T(512)S(1)}, ...), branch_computations={%region_5.5_spmd, %region_6.8_spmd} | conditional | flops 823994240 | bytes 24062050 | solution.py:55
  174.8 2.6 bitcast_add_fusion
  180.1 6.3 %conditional.3 = ((f32[384,1,8]{0,2,1:T(8,128)S(1)}, f32[384,1,8]{0,2,1:T(8,128)S(1)}, f32[384,1,8,128]{0,3,2,1:T(8,128)S(1)})) conditional(s32[]{:T(128)} %convert_element_type.48, (f32[384,1,8]{0,2,1:T(8,128)S(1)}, f32[384,1,8]{0,2,1:T(8,128)S(1)}, f32[384,1,8,128]{0,3,2,1:T(8,128)S(1)}) %tuple.75, (s32[]{:T(128)}, s32[384]{0:T(512)S(1)}, ...), branch_computations={%region_5.5_spmd, %region_6.8_spmd} | conditional | flops 823994240 | bytes 24062050 | solution.py:55
  182.4 2.6 bitcast_add_fusion
  201.1 9.8 %fusion.19 = bf16[5120,384]{0,1:T(8,128)(2,1)} fusion(bf16[384,1024]{0,1:T(8,128)(2,1)S(1)} %bitcast.63, bf16[1024,5120]{1,0:T(8,128)(2,1)} %param.13), kind=kOutput, calls=%fused_computation.27 | convolution fusion | flops 4028497920 | bytes 15204352 | tf_op jit(solution)/shard_map/dot_general | solution.py:104
  210.9 6.3 %copy.27 = bf16[5120,384]{1,0:T(8,128)(2,1)} copy(bf16[5120,384]{0,1:T(8,128)(2,1)} %fusion.19) | data formatting | bytes 7864320
  217.2 57.4 %reduce-scatter.4.cloned.1.call-done = bf16[640,384]{1,0:T(8,128)(2,1)} async-done(((bf16[5120,384]{1,0:T(8,128)(2,1)}), bf16[640,384]{1,0:T(8,128)(2,1)}) %reduce-scatter.4.cloned.1.call-update) | async-done | bytes 491536
  (139 shorter events, 38.3 us)
Async XLA Ops:
  6.5 93.4 %all-gather.2.cloned.1.call-start = ((), (), s32[]{:S(2)}) async-start(), calls=%async_computation.1 | async-start | bytes 6488064 | tf_op jit(solution)/shard_map/all_gather | solution.py:99
  8.2 266.5 %reduce-scatter.4.cloned.1.call-start = ((), (), s32[]{:S(2)}) async-start(), calls=%async_computation.2 | async-start | bytes 4423680
Sparse Core Ops, SparseCore 0:
  9.9 89.9 all-gather.1
  217.4 57.2 reduce-scatter.3
where the time goes:
time: 285 us; the launch traced here: 284 us
  waiting for transfers between devices  144 us (51%)
  matrix products  61.2 us (21%)
  loops' own time  32.5 us (11%)
  other arithmetic  21 us (7%)
  between operations  13.5 us (5%)
  local copies, waits for them, and re-layouts  11.1 us (4%)
    all_gather x1, waiting for transfers between devices, local(): lax.all_gather(stacked, 'ctx', axis=0, tiled=True)  86.8 us
    unnamed x3, waiting for transfers between devices  57.5 us
    another operation x1, loops' own time, sweep(): return lax.fori_loop(0, total_keys // key_block, visit, carry_state)  31.3 us
    dot_general x11, matrix products, attend(): jnp.einsum('rgjk,kgd->rgjd', weights.astype(jnp.bfloat16), value_mat, pre...  29 us
    dot_general x11, matrix products, attend(): jnp.einsum('rgjd,kgd->rgjk', query_mat, key_mat, preferred_element_type=j...  22.4 us
    reduce_sum x11, other arithmetic, attend(): weight_total = weight_total * rescale + jnp.sum(weights, axis=-1)  14.2 us
    unnamed x4, local copies, waits for them, and re-layouts  10.1 us
    dot_general x1, matrix products, local(): lax.dot_general(out_weight, result_rows, (((0,), (1,)), ((), ())), prefer...  9.83 us
  transfers between devices with their start and end apart: 2, of which 2 were waited for; matrix products, arithmetic and copies ran while one was open for 2% of the time, Pallas kernels for 0%

commit v1 on v0

v1 whole, which is shorter than its diff:
```python
import functools
import math

import jax
import jax.numpy as jnp
from jax import lax
from jax.experimental import pallas as pl
from jax.experimental.pallas import tpu as pltpu
from jax.sharding import PartitionSpec as P

MESH = pl.DeviceIdType.MESH
HEAD = 128
GROUP = 8
ROWS = 384
CHUNK = 512
NY, NZ, NX, NK = 4, 8, 4, 2
WIDE = 640
COLS = GROUP * ROWS
SCALE = math.log2(math.e) / math.sqrt(HEAD)
BIG = 262144.0
LOW = -1e30

ORDER = ((0,), (8,), (16,), (1, 7), (9, 17), (2, 15), (6, 18), (10, 14), (3, 5), (11, 13), (4, 12))
TICKS = (
    (
        (1, 1, 1, 0, 1), (1, 3, 0, 3, 0), (1, 1, 0, 0, 1), (1, 2, 1, 1, 0), (1, 2, 0, 1, 0), (1, 0, 1, 0, 7),
        (1, 0, 0, 0, 7),
    ),
    (
        (0, 0, 3, 0), (1, 3, 0, 2, 0), (0, 1, 0, 1), (0, 1, 1, 0), (0, 1, 0, 7), (1, 1, 1, 0, 2),
        (1, 1, 1, 1, 1), (1, 0, 1, 1, 7), (1, 0, 1, 0, 6), (1, 2, 1, 2, 0), (0, 0, 0, 1), (0, 0, 1, 0),
        (0, 0, 0, 7), (1, 3, 0, 3, 7), (1, 2, 0, 1, 1), (1, 1, 0, 0, 2), (1, 3, 0, 3, 1), (1, 0, 0, 0, 6),
        (1, 2, 0, 1, 7),
    ),
    (
        (0, 0, 2, 0), (0, 0, 3, 7), (0, 1, 0, 2), (0, 1, 1, 7), (0, 1, 2, 0), (1, 2, 1, 2, 7),
        (1, 3, 0, 2, 7), (1, 0, 1, 1, 6), (1, 1, 1, 0, 3),
    ),
    (
        (0, 0, 3, 1), (0, 0, 1, 1), (1, 3, 0, 2, 1), (0, 1, 1, 1), (0, 1, 0, 6), (0, 0, 1, 7),
        (1, 2, 1, 2, 1), (1, 1, 1, 1, 2), (1, 0, 1, 0, 5),
    ),
    (
        (0, 0, 2, 7), (0, 0, 0, 2), (0, 0, 0, 6), (0, 0, 2, 1), (0, 1, 2, 7), (1, 1, 0, 0, 3),
        (1, 0, 1, 2, 6), (1, 2, 0, 1, 6), (1, 2, 0, 1, 2), (1, 1, 0, 2, 2), (1, 0, 0, 0, 5), (1, 3, 0, 3, 6),
        (3,),
    ),
    (
        (0, 1, 1, 6), (0, 1, 0, 3), (0, 1, 2, 1), (0, 0, 3, 6), (0, 1, 1, 2), (0, 1, 0, 5), (2,),
        (0, 0, 1, 6), (1, 1, 1, 2, 2), (1, 2, 1, 1, 3), (1, 3, 0, 2, 6), (1, 2, 1, 1, 5), (1, 1, 1, 0, 4),
    ),
    (
        (0, 0, 0, 3), (0, 0, 1, 2), (0, 1, 2, 6), (0, 0, 2, 2), (0, 0, 2, 6), (1, 2, 0, 1, 3),
        (1, 1, 0, 0, 4), (1, 1, 0, 2, 3), (1, 0, 1, 2, 5),
    ),
    (
        (0, 0, 0, 5), (0, 1, 1, 3), (0, 1, 2, 2), (0, 1, 1, 5), (1, 0, 1, 1, 4), (1, 2, 0, 1, 5),
        (1, 3, 0, 3, 5), (1, 2, 1, 2, 3),
    ),
    (
        (0, 1, 2, 5), (0, 1, 0, 4), (0, 0, 1, 3), (0, 0, 0, 4), (0, 0, 1, 5), (0, 0, 3, 5), (0, 0, 2, 3),
        (1, 0, 1, 2, 4), (1, 3, 0, 2, 5), (1, 1, 0, 2, 4), (1, 2, 0, 1, 4),
    ),
    (
        (0, 1, 1, 4), (0, 1, 2, 3), (0, 0, 2, 5), (0, 0, 2, 4), (0, 0, 1, 4),
    ),
    (
        (0, 1, 2, 4),
    ),
)
MESSAGES = tuple(item[1:] for tick in TICKS for item in tick if item[0] == 1)


def pick(index, numbers):
    value = jnp.int32(numbers[0])
    for at, number in enumerate(numbers[1:], 1):
        value = jnp.where(index == at, jnp.int32(number), value)
    return value


def kernel(
    q_ref, k_ref, v_ref, len_ref, w_ref, out_ref,
    qt, kv, acc, top, qpos, firsts, lasts, wts, att, far, near_r, near_l, mid_l, mid_r, in_l, in_r,
    kv_send, kv_recv, sp_send, sp_recv, w_local, w_send, w_recv, a_send, a_recv, x_send, x_recv,
):
    ctx, tp = lax.axis_index("ctx"), lax.axis_index("tp")
    y, z = ctx // NZ, lax.rem(ctx, NZ)
    x, core = tp // NK, lax.rem(tp, NK)
    z_next = (y * NZ + lax.rem(z + 1, NZ), tp)
    z_back = (y * NZ + lax.rem(z + NZ - 1, NZ), tp)
    y_next = (lax.rem(y + 1, NY) * NZ + z, tp)
    y_back = (lax.rem(y + NY - 1, NY) * NZ + z, tp)
    x_next = (ctx, lax.rem(x + 1, NX) * NK + core)
    x_back = (ctx, lax.rem(x + NX - 1, NX) * NK + core)
    other = (ctx, x * NK + 1 - core)
    links = (z_next, z_back, y_next, y_back)
    shift = ((0, 1), (0, -1), (-1, 0), (1, 0))

    kv[3, 6:8, 1:3] = jnp.zeros((2, 2, 2 * HEAD, HEAD), jnp.bfloat16)
    barrier = pltpu.get_barrier_semaphore()
    for device in links + (x_next, x_back, other):
        pl.semaphore_signal(barrier, inc=1, device_id=device, device_id_type=MESH)

    values_t = v_ref[...].astype(jnp.float32).T.astype(jnp.bfloat16)
    for c in range(3):
        kv[0, z, c, 0:HEAD, :] = k_ref[c * HEAD:(c + 1) * HEAD, :]
        kv[0, z, c, HEAD:, :] = values_t[:, c * HEAD:(c + 1) * HEAD]

    def message(link, part, row, column):
        piece = pl.ds(0, 1) if part == 0 else pl.ds(1, 2)
        dy, dz = shift[link]
        held = (row + dy) % NY
        col = lax.rem(z + (column + dz) + 2 * NZ, NZ)
        return pltpu.make_async_remote_copy(
            src_ref=kv.at[held, col, piece],
            dst_ref=kv.at[row, col, piece],
            send_sem=kv_send.at[part, row, column],
            recv_sem=kv_recv.at[part, row, column],
            device_id=links[link],
            device_id_type=MESH,
        )

    def arrival(part, row, column):
        piece = pl.ds(0, 1) if part == 0 else pl.ds(1, 2)
        slot = kv.at[row, lax.rem(z + column, NZ), piece]
        return pltpu.make_async_remote_copy(
            src_ref=slot,
            dst_ref=slot,
            send_sem=kv_send.at[part, row, column],
            recv_sem=kv_recv.at[part, row, column],
            device_id=z_next,
            device_id_type=MESH,
        )

    def special(at):
        return pltpu.make_async_remote_copy(
            src_ref=kv.at[0, 6 + at, pl.ds(1, 2)],
            dst_ref=kv.at[3, 6 + at, pl.ds(1, 2)],
            send_sem=sp_send.at[at],
            recv_sem=sp_recv.at[at],
            device_id=y_back,
            device_id_type=MESH,
        )

    sends_special = (y == 0) & (z < 2)
    takes_special = (y == NY - 1) & (z < 2)

    def act(item):
        if item[0] == 0:
            arrival(*item[1:]).wait_recv()
        elif item[0] == 1:
            message(*item[1:]).start()
        elif item[0] == 2:
            @pl.when(sends_special)
            def _():
                for at in range(2):
                    special(at).start()
        else:
            @pl.when(takes_special)
            def _():
                for at in range(2):
                    special(at).wait_recv()

    pl.semaphore_wait(barrier, 7)
    for item in TICKS[0]:
        act(item)

    def weight_columns(xx, half):
        return pl.ds(pl.multiple_of(xx * (2 * WIDE) + half * WIDE, HEAD), WIDE)

    def weight_keep(xx):
        return pltpu.make_async_copy(w_ref.at[:, weight_columns(xx, core)], wts.at[core, xx], w_local.at[xx])

    def weight_give(xx):
        return pltpu.make_async_remote_copy(
            src_ref=w_ref.at[:, weight_columns(xx, 1 - core)],
            dst_ref=wts.at[core, xx],
            send_sem=w_send.at[xx],
            recv_sem=w_recv.at[xx],
            device_id=other,
            device_id_type=MESH,
        )

    for xx in range(NX):
        weight_keep(xx).start()
        weight_give(xx).start()

    lane = lax.broadcasted_iota(jnp.int32, (8, HEAD), 1)
    sub = lax.broadcasted_iota(jnp.int32, (HEAD, ROWS), 0)
    first_l = jnp.where(lane == HEAD - 1, -(1 << 30), 0)
    last_l = jnp.zeros_like(lane)
    first_s, last_s = jnp.zeros_like(sub), jnp.zeros_like(sub)
    begin = jnp.int32(0)
    for d in range(24):
        end = begin + len_ref[d]
        first_l, last_l = jnp.where(lane == d, begin, first_l), jnp.where(lane == d, end, last_l)
        first_s, last_s = jnp.where(sub == d, begin, first_s), jnp.where(sub == d, end, last_s)
        begin = end
    firsts[...] = first_l
    lasts[...] = last_l
    own = ctx * ROWS + lax.broadcasted_iota(jnp.int32, (HEAD, ROWS), 1)
    apart = jnp.where((own >= first_s) & (own < last_s), 0.0, -BIG).astype(jnp.bfloat16)
    for h in range(GROUP):
        span = slice(h * ROWS, (h + 1) * ROWS)
        qt[0:HEAD, span] = q_ref[:, h * HEAD:(h + 1) * HEAD].astype(jnp.float32).T.astype(jnp.bfloat16)
        qt[HEAD:, span] = apart
        qpos[:, span] = own[0:8]
    top[...] = jnp.full_like(top, LOW)
    acc[...] = jnp.zeros_like(acc)

    def block(delta):
        row = (delta - z + NZ - 1) // NZ
        col = lax.rem(z - delta + 3 * NZ, NZ)
        held = kv[row, col]
        pos = (ctx - delta) * ROWS + lax.broadcasted_iota(jnp.int32, (ROWS, HEAD), 0)
        same = jnp.where((pos >= firsts[0:1, :]) & (pos < lasts[0:1, :]), 1.0, 0.0).astype(jnp.bfloat16)
        keys = jnp.concatenate([held[c, 0:HEAD] for c in range(3)], axis=0)
        vals = jnp.concatenate([held[c, HEAD:] for c in range(3)], axis=1)
        return jnp.concatenate([keys, same], axis=1), vals

    def attend(deltas, causal):
        parts = [block(delta) for delta in deltas]
        keys = jnp.concatenate([part[0] for part in parts], axis=0)
        vals = jnp.concatenate([part[1] for part in parts], axis=1)
        count = keys.shape[0]
        vals = jnp.concatenate([vals, jnp.ones((16, count), jnp.bfloat16)], axis=0)

        def score(j):
            span = slice(j * CHUNK, (j + 1) * CHUNK)
            got = jnp.dot(keys, qt[:, span], preferred_element_type=jnp.float32)
            if causal:
                pos = (ctx - deltas[0]) * ROWS + lax.broadcasted_iota(jnp.int32, (count, CHUNK), 0)
                got = jnp.where(pos <= qpos[0:1, span], got, -BIG)
            return got

        def soften(j, got):
            span = slice(j * CHUNK, (j + 1) * CHUNK)
            old = top[0:1, span]
            new = jnp.maximum(old, jnp.max(got, axis=0, keepdims=True))
            top[0:1, span] = new
            return jnp.exp2((got - new) * SCALE).astype(jnp.bfloat16), jnp.exp2((old - new) * SCALE)

        def gather(j, weights, fade):
            span = slice(j * CHUNK, (j + 1) * CHUNK)
            acc[:, span] = acc[:, span] * fade + jnp.dot(vals, weights, preferred_element_type=jnp.float32)

        steps = COLS // CHUNK
        got, held = score(0), None
        for j in range(steps):
            ahead = score(j + 1) if j + 1 < steps else None
            soft = soften(j, got)
            if held is not None:
                gather(j - 1, *held)
            got, held = ahead, soft
        gather(steps - 1, *held)

    def step(i, carry):
        for at in range(1, len(ORDER)):
            @pl.when(i == at)
            def _(at=at):
                for item in TICKS[at]:
                    act(item)
        one = pick(i, [min(group) for group in ORDER])
        two = pick(i, [max(group) for group in ORDER])

        @pl.when((one == two) & (ctx >= one))
        def _():
            attend((one,), True)

        @pl.when((one != two) & (ctx >= one))
        def _():
            attend((one, two), False)

        return carry

    lax.fori_loop(0, len(ORDER), step, 0)

    for h in range(GROUP):
        span = slice(h * ROWS, (h + 1) * ROWS)
        rows = acc[0:HEAD, span] / acc[HEAD:HEAD + 1, span]
        att[core, :, h * HEAD:(h + 1) * HEAD] = rows.T.astype(jnp.bfloat16)
    swap = pltpu.make_async_remote_copy(
        src_ref=att.at[core], dst_ref=att.at[core], send_sem=a_send, recv_sem=a_recv, device_id=other, device_id_type=MESH,
    )
    swap.start()
    for xx in range(NX):
        weight_keep(xx).wait()
        weight_give(xx).wait()
    swap.wait()

    half = ROWS // 2
    lower, upper = pl.ds(0, half), pl.ds(half, half)

    def project(xx):
        total = jnp.dot(att[0], wts[0, xx], preferred_element_type=jnp.float32)
        return total + jnp.dot(att[1], wts[1, xx], preferred_element_type=jnp.float32)

    def along(at, src, dst, device):
        return pltpu.make_async_remote_copy(
            src_ref=src, dst_ref=dst, send_sem=x_send.at[at], recv_sem=x_recv.at[at], device_id=device, device_id_type=MESH,
        )

    far_up = along(0, far.at[lower], mid_l, x_next)
    far_down = along(1, far.at[upper], mid_r, x_back)
    up_a = along(2, near_r.at[upper], in_l.at[upper], x_next)
    down_a = along(3, near_l.at[lower], in_r.at[lower], x_back)
    up_b = along(4, near_r.at[lower], in_l.at[lower], x_next)
    down_b = along(5, near_l.at[upper], in_r.at[upper], x_back)

    far[...] = project(lax.rem(x + 2, NX)).astype(jnp.bfloat16)
    far_up.start()
    far_down.start()
    near_r[...] = project(lax.rem(x + 1, NX)).astype(jnp.bfloat16)
    up_a.start()
    near_l[...] = project(lax.rem(x + NX - 1, NX)).astype(jnp.bfloat16)
    down_a.start()
    far_up.wait_recv()
    near_r[0:half] = (near_r[0:half].astype(jnp.float32) + mid_l[...].astype(jnp.float32)).astype(jnp.bfloat16)
    up_b.start()
    far_down.wait_recv()
    near_l[half:] = (near_l[half:].astype(jnp.float32) + mid_r[...].astype(jnp.float32)).astype(jnp.bfloat16)
    down_b.start()
    mine = project(x)
    for copy in (up_a, down_a, up_b, down_b):
        copy.wait_recv()
    out_ref[...] = (mine + in_l[...].astype(jnp.float32) + in_r[...].astype(jnp.float32)).astype(jnp.bfloat16)
    for copy in (far_up, far_down, up_a, down_a, up_b, down_b):
        copy.wait_send()
    for item in MESSAGES:
        message(*item).wait_send()

    @pl.when(sends_special)
    def _():
        for at in range(2):
            special(at).wait_send()


def local(queries, keys, values, doc_lengths, out_weight):
    vmem = pl.BlockSpec(memory_space=pltpu.VMEM)
    bf16, f32 = jnp.bfloat16, jnp.float32
    dma = pltpu.SemaphoreType.DMA
    return pl.pallas_call(
        kernel,
        out_shape=jax.ShapeDtypeStruct((ROWS, WIDE), bf16),
        in_specs=[vmem, vmem, vmem, pl.BlockSpec(memory_space=pltpu.SMEM), pl.BlockSpec(memory_space=pl.ANY)],
        out_specs=vmem,
        scratch_shapes=[
            pltpu.VMEM((2 * HEAD, COLS), bf16),
            pltpu.VMEM((NY, NZ, 3, 2 * HEAD, HEAD), bf16),
            pltpu.VMEM((HEAD + 16, COLS), f32),
            pltpu.VMEM((8, COLS), f32),
            pltpu.VMEM((8, COLS), jnp.int32),
            pltpu.VMEM((8, HEAD), jnp.int32),
            pltpu.VMEM((8, HEAD), jnp.int32),
            pltpu.VMEM((NK, NX, GROUP * HEAD, WIDE), bf16),
            pltpu.VMEM((NK, ROWS, GROUP * HEAD), bf16),
            pltpu.VMEM((ROWS, WIDE), bf16),
            pltpu.VMEM((ROWS, WIDE), bf16),
            pltpu.VMEM((ROWS, WIDE), bf16),
            pltpu.VMEM((ROWS // 2, WIDE), bf16),
            pltpu.VMEM((ROWS // 2, WIDE), bf16),
            pltpu.VMEM((ROWS, WIDE), bf16),
            pltpu.VMEM((ROWS, WIDE), bf16),
            dma((2, NY, NZ)),
            dma((2, NY, NZ)),
            dma((2,)),
            dma((2,)),
            dma((NX,)),
            dma((NX,)),
            dma((NX,)),
            dma,
            dma,
            dma((6,)),
            dma((6,)),
        ],
        compiler_params=pltpu.CompilerParams(
            collective_id=0, has_side_effects=True, vmem_limit_bytes=60 << 20
        ),
    )(queries, keys, values, doc_lengths, out_weight)


def solution(mesh):
    in_specs = (P("ctx", "tp"), P("ctx", "tp"), P("ctx", "tp"), P(), P("tp", None))
    out_specs = P("ctx", "tp")
    return jax.shard_map(local, mesh=mesh, in_specs=in_specs, out_specs=out_specs, check_vma=False)
```

time: 285 us -> 86.2 us (0.30)
  waiting for transfers between devices: 144 us -> 0 us
  Pallas kernels: 0 us -> 84.1 us
  matrix products: 61.2 us -> 0 us
  loops' own time: 32.5 us -> 0 us
  other arithmetic: 21 us -> 0 us
  between operations: 13.5 us -> 0.01 us
  local copies, waits for them, and re-layouts: 11.1 us -> 1.85 us
    all_gather x1 -> x0, waiting for transfers between devices: 86.8 us -> none  [local(): lax.all_gather(stacked, 'ctx', axis=0, tiled=True)]
    pallas_call x0 -> x1, Pallas kernels: none -> 84.1 us  [local(): pl.pallas_call(kernel, out_shape=jax.ShapeDtypeStruct((ROWS, WIDE), bf16)...]
    dot_general x23 -> x0, matrix products: 61.2 us -> none  [the longest x11 29 us: attend(): jnp.einsum('rgjk,kgd->rgjd', weights.astype(jnp.bfloat16), value_mat, pre...]
    unnamed x3 -> x0, waiting for transfers between devices: 57.5 us -> none
    another operation x25 -> x0, loops' own time: 32.5 us -> none  [the longest x1 31.3 us: sweep(): return lax.fori_loop(0, total_keys // key_block, visit, carry_state)]
    reduce_sum x11 -> x0, other arithmetic: 14.2 us -> none  [attend(): weight_total = weight_total * rescale + jnp.sum(weights, axis=-1)]
    unnamed x4 -> x1, local copies, waits for them, and re-layouts: 10.1 us -> 1.85 us
  transfers between devices with their start and end apart: 2 -> 0, of which waited for: 2 -> 0; matrix products, arithmetic and copies ran while one was open for 2% -> 0% of each run, Pallas kernels for 0% -> 0%
where the time goes in v1:
time: 86.2 us; the launch traced here: 86 us
  Pallas kernels  84.1 us (98%)
  local copies, waits for them, and re-layouts  1.85 us (2%)
    pallas_call x1, Pallas kernels, local(): pl.pallas_call(kernel, out_shape=jax.ShapeDtypeStruct((ROWS, WIDE), bf16)...  84.1 us
    unnamed x1, local copies, waits for them, and re-layouts  1.85 us

profile of v1, /device:TPU:16, one launch (start us, length us, event | category | flops | bytes accessed | tf_op | source)
XLA Modules:
  0.0 86.0 jit_solution(3859277222041460509)
XLA Ops:
  0.0 84.1 %shard_map.55 = bf16[384,640]{1,0:T(8,128)(2,1)} custom-call(bf16[384,1024]{1,0:T(8,128)(2,1)} %q_ref.1, bf16[384,128]{1,0:T(8,128)(2,1)} %k_ref.1, bf16[384,128]{1,0:T(8,128)(2,1)} %v_ref.1, s32[24]{0:T(128)} %len_ref.1, bf16[1024,5120]{1,0:T(8,128)(2,1)} %w_ref.1), custom_call_target="tpu_custom_call" | custom-call | tf_op jit(solution)/shard_map/pallas_call | solution.py:342
  84.1 1.9 %copy.7 = bf16[384,640]{1,0:T(8,128)(2,1)} copy(bf16[384,640]{1,0:T(8,128)(2,1)} %shard_map.55) | data formatting | bytes 983040

commit v2 on v1

--- a/solution.py
+++ b/solution.py
@@ -16,11 +16,15 @@
 NY, NZ, NX, NK = 4, 8, 4, 2
 WIDE = 640
 COLS = GROUP * ROWS
+TILES = 3
+TILE = ROWS // TILES
+SPAN = GROUP * TILE
 SCALE = math.log2(math.e) / math.sqrt(HEAD)
 BIG = 262144.0
 LOW = -1e30
 
-ORDER = ((0,), (8,), (16,), (1, 7), (9, 17), (2, 15), (6, 18), (10, 14), (3, 5), (11, 13), (4, 12))
+ORDER = ((0,), (8,), (16,), (1, 7), (9, 17), (2, 15), (6, 18), (10, 14), (3, 5))
+LAST = (4, 11, 12, 13)
 TICKS = (
     (
         (1, 1, 1, 0, 1), (1, 3, 0, 3, 0), (1, 1, 0, 0, 1), (1, 2, 1, 1, 0), (1, 2, 0, 1, 0), (1, 0, 1, 0, 7),
@@ -62,10 +66,7 @@
         (1, 0, 1, 2, 4), (1, 3, 0, 2, 5), (1, 1, 0, 2, 4), (1, 2, 0, 1, 4),
     ),
     (
-        (0, 1, 1, 4), (0, 1, 2, 3), (0, 0, 2, 5), (0, 0, 2, 4), (0, 0, 1, 4),
-    ),
-    (
-        (0, 1, 2, 4),
+        (0, 1, 1, 4), (0, 1, 2, 3), (0, 0, 2, 5), (0, 0, 2, 4), (0, 0, 1, 4), (0, 1, 2, 4),
     ),
 )
 MESSAGES = tuple(item[1:] for tick in TICKS for item in tick if item[0] == 1)
@@ -80,7 +81,7 @@
 
 def kernel(
     q_ref, k_ref, v_ref, len_ref, w_ref, out_ref,
-    qt, kv, acc, top, qpos, firsts, lasts, wts, att, far, near_r, near_l, mid_l, mid_r, in_l, in_r,
+    qt, kv, acc, top, qpos, firsts, lasts, wts, att, far, near_r, near_l, mid_l, mid_r, in_l, in_r, mine,
     kv_send, kv_recv, sp_send, sp_recv, w_local, w_send, w_recv, a_send, a_recv, x_send, x_recv,
 ):
     ctx, tp = lax.axis_index("ctx"), lax.axis_index("tp")
@@ -201,10 +202,13 @@
     own = ctx * ROWS + lax.broadcasted_iota(jnp.int32, (HEAD, ROWS), 1)
     apart = jnp.where((own >= first_s) & (own < last_s), 0.0, -BIG).astype(jnp.bfloat16)
     for h in range(GROUP):
-        span = slice(h * ROWS, (h + 1) * ROWS)
-        qt[0:HEAD, span] = q_ref[:, h * HEAD:(h + 1) * HEAD].astype(jnp.float32).T.astype(jnp.bfloat16)
-        qt[HEAD:, span] = apart
-        qpos[:, span] = own[0:8]
+        turned = q_ref[:, h * HEAD:(h + 1) * HEAD].astype(jnp.float32).T.astype(jnp.bfloat16)
+        for t in range(TILES):
+            span = slice(t * SPAN + h * TILE, t * SPAN + (h + 1) * TILE)
+            rows = slice(t * TILE, (t + 1) * TILE)
+            qt[0:HEAD, span] = turned[:, rows]
+            qt[HEAD:, span] = apart[:, rows]
+            qpos[:, span] = own[0:8, rows]
     top[...] = jnp.full_like(top, LOW)
     acc[...] = jnp.zeros_like(acc)
 
@@ -218,15 +222,20 @@
         vals = jnp.concatenate([held[c, HEAD:] for c in range(3)], axis=1)
         return jnp.concatenate([keys, same], axis=1), vals
 
-    def attend(deltas, causal):
+    def attend(deltas, causal, base, steps):
         parts = [block(delta) for delta in deltas]
         keys = jnp.concatenate([part[0] for part in parts], axis=0)
         vals = jnp.concatenate([part[1] for part in parts], axis=1)
         count = keys.shape[0]
         vals = jnp.concatenate([vals, jnp.ones((16, count), jnp.bfloat16)], axis=0)
 
+        def span_of(j):
+            if isinstance(base, int):
+                return slice(base + j * CHUNK, base + (j + 1) * CHUNK)
+            return pl.ds(pl.multiple_of(base + j * CHUNK, CHUNK), CHUNK)
+
         def score(j):
-            span = slice(j * CHUNK, (j + 1) * CHUNK)
+            span = span_of(j)
             got = jnp.dot(keys, qt[:, span], preferred_element_type=jnp.float32)
             if causal:
                 pos = (ctx - deltas[0]) * ROWS + lax.broadcasted_iota(jnp.int32, (count, CHUNK), 0)
@@ -234,17 +243,16 @@
             return got
 
         def soften(j, got):
-            span = slice(j * CHUNK, (j + 1) * CHUNK)
+            span = span_of(j)
             old = top[0:1, span]
             new = jnp.maximum(old, jnp.max(got, axis=0, keepdims=True))
             top[0:1, span] = new
             return jnp.exp2((got - new) * SCALE).astype(jnp.bfloat16), jnp.exp2((old - new) * SCALE)
 
         def gather(j, weights, fade):
-            span = slice(j * CHUNK, (j + 1) * CHUNK)
+            span = span_of(j)
             acc[:, span] = acc[:, span] * fade + jnp.dot(vals, weights, preferred_element_type=jnp.float32)
 
-        steps = COLS // CHUNK
         got, held = score(0), None
         for j in range(steps):
             ahead = score(j + 1) if j + 1 < steps else None
@@ -265,67 +273,106 @@
 
         @pl.when((one == two) & (ctx >= one))
         def _():
-            attend((one,), True)
+            attend((one,), True, 0, COLS // CHUNK)
 
         @pl.when((one != two) & (ctx >= one))
         def _():
-            attend((one, two), False)
+            attend((one, two), False, 0, COLS // CHUNK)
 
         return carry
 
     lax.fori_loop(0, len(ORDER), step, 0)
 
-    for h in range(GROUP):
-        span = slice(h * ROWS, (h + 1) * ROWS)
-        rows = acc[0:HEAD, span] / acc[HEAD:HEAD + 1, span]
-        att[core, :, h * HEAD:(h + 1) * HEAD] = rows.T.astype(jnp.bfloat16)
-    swap = pltpu.make_async_remote_copy(
-        src_ref=att.at[core], dst_ref=att.at[core], send_sem=a_send, recv_sem=a_recv, device_id=other, device_id_type=MESH,
-    )
-    swap.start()
+    for item in TICKS[len(ORDER)]:
+        act(item)
     for xx in range(NX):
         weight_keep(xx).wait()
         weight_give(xx).wait()
-    swap.wait()
-
-    half = ROWS // 2
+
+    half = TILE // 2
+
+    def swap(t):
+        held = att.at[core, t]
+        return pltpu.make_async_remote_copy(
+            src_ref=held, dst_ref=held, send_sem=a_send.at[t], recv_sem=a_recv.at[t], device_id=other, device_id_type=MESH,
+        )
+
+    def along(t, at, src, dst, device):
+        return pltpu.make_async_remote_copy(
+            src_ref=src,
+            dst_ref=dst,
+            send_sem=x_send.at[t, at],
+            recv_sem=x_recv.at[t, at],
+            device_id=device,
+            device_id_type=MESH,
+        )
+
     lower, upper = pl.ds(0, half), pl.ds(half, half)
 
-    def project(xx):
-        total = jnp.dot(att[0], wts[0, xx], preferred_element_type=jnp.float32)
-        return total + jnp.dot(att[1], wts[1, xx], preferred_element_type=jnp.float32)
-
-    def along(at, src, dst, device):
-        return pltpu.make_async_remote_copy(
-            src_ref=src, dst_ref=dst, send_sem=x_send.at[at], recv_sem=x_recv.at[at], device_id=device, device_id_type=MESH,
-        )
-
-    far_up = along(0, far.at[lower], mid_l, x_next)
-    far_down = along(1, far.at[upper], mid_r, x_back)
-    up_a = along(2, near_r.at[upper], in_l.at[upper], x_next)
-    down_a = along(3, near_l.at[lower], in_r.at[lower], x_back)
-    up_b = along(4, near_r.at[lower], in_l.at[lower], x_next)
-    down_b = along(5, near_l.at[upper], in_r.at[upper], x_back)
-
-    far[...] = project(lax.rem(x + 2, NX)).astype(jnp.bfloat16)
-    far_up.start()
-    far_down.start()
-    near_r[...] = project(lax.rem(x + 1, NX)).astype(jnp.bfloat16)
-    up_a.start()
-    near_l[...] = project(lax.rem(x + NX - 1, NX)).astype(jnp.bfloat16)
-    down_a.start()
-    far_up.wait_recv()
-    near_r[0:half] = (near_r[0:half].astype(jnp.float32) + mid_l[...].astype(jnp.float32)).astype(jnp.bfloat16)
-    up_b.start()
-    far_down.wait_recv()
-    near_l[half:] = (near_l[half:].astype(jnp.float32) + mid_r[...].astype(jnp.float32)).astype(jnp.bfloat16)
-    down_b.start()
-    mine = project(x)
-    for copy in (up_a, down_a, up_b, down_b):
-        copy.wait_recv()
-    out_ref[...] = (mine + in_l[...].astype(jnp.float32) + in_r[...].astype(jnp.float32)).astype(jnp.bfloat16)
-    for copy in (far_up, far_down, up_a, down_a, up_b, down_b):
-        copy.wait_send()
+    def copies(t):
+        return (
+            along(t, 0, far.at[t, lower], mid_l.at[t], x_next),
+            along(t, 1, far.at[t, upper], mid_r.at[t], x_back),
+            along(t, 2, near_r.at[t, upper], in_l.at[t, upper], x_next),
+            along(t, 3, near_l.at[t, lower], in_r.at[t, lower], x_back),
+            along(t, 4, near_r.at[t, lower], in_l.at[t, lower], x_next),
+            along(t, 5, near_l.at[t, upper], in_r.at[t, upper], x_back),
+        )
+
+    def pass_on(t):
+        far_up, far_down, _, _, up, down = copies(t)
+        far_up.wait_recv()
+        near_r[t, 0:half] = (near_r[t, 0:half].astype(jnp.float32) + mid_l[t].astype(jnp.float32)).astype(jnp.bfloat16)
+        up.start()
+        far_down.wait_recv()
+        near_l[t, half:] = (near_l[t, half:].astype(jnp.float32) + mid_r[t].astype(jnp.float32)).astype(jnp.bfloat16)
+        down.start()
+
+    def finish(t, carry):
+        base = t * SPAN
+
+        @pl.when(ctx >= min(LAST))
+        def _():
+            attend(LAST, False, base, SPAN // CHUNK)
+
+        for h in range(GROUP):
+            span = pl.ds(pl.multiple_of(base + h * TILE, TILE), TILE)
+            rows = acc[0:HEAD, span] / acc[HEAD:HEAD + 1, span]
+            att[core, t, :, h * HEAD:(h + 1) * HEAD] = rows.T.astype(jnp.bfloat16)
+        swap(t).start()
+
+        @pl.when(t > 0)
+        def _():
+            pass_on(t - 1)
+
+        targets = [lax.rem(x + step, NX) for step in (2, 1, 3, 0)]
+        sums = [jnp.dot(att[core, t], wts[core, xx], preferred_element_type=jnp.float32) for xx in targets]
+        swap(t).wait()
+
+        def whole(at):
+            return sums[at] + jnp.dot(att[1 - core, t], wts[1 - core, targets[at]], preferred_element_type=jnp.float32)
+
+        far_up, far_down, up, down, _, _ = copies(t)
+        far[t] = whole(0).astype(jnp.bfloat16)
+        far_up.start()
+        far_down.start()
+        near_r[t] = whole(1).astype(jnp.bfloat16)
+        up.start()
+        near_l[t] = whole(2).astype(jnp.bfloat16)
+        down.start()
+        mine[t] = whole(3)
+        return carry
+
+    lax.fori_loop(0, TILES, finish, 0)
+    pass_on(TILES - 1)
+    for t in range(TILES):
+        for copy in copies(t)[2:]:
+            copy.wait_recv()
+        total = mine[t] + in_l[t].astype(jnp.float32) + in_r[t].astype(jnp.float32)
+        out_ref[t * TILE:(t + 1) * TILE] = total.astype(jnp.bfloat16)
+    for t in range(TILES):
+        for copy in copies(t):
+            copy.wait_send()
     for item in MESSAGES:
         message(*item).wait_send()
 
@@ -353,14 +400,15 @@
             pltpu.VMEM((8, HEAD), jnp.int32),
             pltpu.VMEM((8, HEAD), jnp.int32),
             pltpu.VMEM((NK, NX, GROUP * HEAD, WIDE), bf16),
-            pltpu.VMEM((NK, ROWS, GROUP * HEAD), bf16),
-            pltpu.VMEM((ROWS, WIDE), bf16),
-            pltpu.VMEM((ROWS, WIDE), bf16),
-            pltpu.VMEM((ROWS, WIDE), bf16),
-            pltpu.VMEM((ROWS // 2, WIDE), bf16),
-            pltpu.VMEM((ROWS // 2, WIDE), bf16),
-            pltpu.VMEM((ROWS, WIDE), bf16),
-            pltpu.VMEM((ROWS, WIDE), bf16),
+            pltpu.VMEM((NK, TILES, TILE, GROUP * HEAD), bf16),
+            pltpu.VMEM((TILES, TILE, WIDE), bf16),
+            pltpu.VMEM((TILES, TILE, WIDE), bf16),
+            pltpu.VMEM((TILES, TILE, WIDE), bf16),
+            pltpu.VMEM((TILES, TILE // 2, WIDE), bf16),
+            pltpu.VMEM((TILES, TILE // 2, WIDE), bf16),
+            pltpu.VMEM((TILES, TILE, WIDE), bf16),
+            pltpu.VMEM((TILES, TILE, WIDE), bf16),
+            pltpu.VMEM((TILES, TILE, WIDE), f32),
             dma((2, NY, NZ)),
             dma((2, NY, NZ)),
             dma((2,)),
@@ -368,10 +416,10 @@
             dma((NX,)),
             dma((NX,)),
             dma((NX,)),
-            dma,
-            dma,
-            dma((6,)),
-            dma((6,)),
+            dma((TILES,)),
+            dma((TILES,)),
+            dma((TILES, 6)),
+            dma((TILES, 6)),
         ],
         compiler_params=pltpu.CompilerParams(
             collective_id=0, has_side_effects=True, vmem_limit_bytes=60 << 20

time: 86.2 us -> 81.9 us (0.950)
  Pallas kernels: 84.1 us -> 79.9 us
    pallas_call x1, Pallas kernels: 84.1 us -> 79.9 us  [local(): pl.pallas_call(kernel, out_shape=jax.ShapeDtypeStruct((ROWS, WIDE), bf16)...]
where the time goes in v2:
time: 81.9 us; the launch traced here: 81.7 us
  Pallas kernels  79.9 us (98%)
  local copies, waits for them, and re-layouts  1.85 us (2%)
    pallas_call x1, Pallas kernels, local(): pl.pallas_call(kernel, out_shape=jax.ShapeDtypeStruct((ROWS, WIDE), bf16)...  79.9 us
    unnamed x1, local copies, waits for them, and re-layouts  1.85 us

profile of v2, /device:TPU:16, one launch (start us, length us, event | category | flops | bytes accessed | tf_op | source)
XLA Modules:
  0.0 81.7 jit_solution(16906559514712899587)
XLA Ops:
  0.0 79.9 %shard_map.55 = bf16[384,640]{1,0:T(8,128)(2,1)} custom-call(bf16[384,1024]{1,0:T(8,128)(2,1)} %q_ref.1, bf16[384,128]{1,0:T(8,128)(2,1)} %k_ref.1, bf16[384,128]{1,0:T(8,128)(2,1)} %v_ref.1, s32[24]{0:T(128)} %len_ref.1, bf16[1024,5120]{1,0:T(8,128)(2,1)} %w_ref.1), custom_call_target="tpu_custom_call" | custom-call | tf_op jit(solution)/shard_map/pallas_call | solution.py:389
  79.9 1.9 %copy.7 = bf16[384,640]{1,0:T(8,128)(2,1)} copy(bf16[384,640]{1,0:T(8,128)(2,1)} %shard_map.55) | data formatting | bytes 983040

commit v3 on v2

--- a/solution.py
+++ b/solution.py
@@ -23,50 +23,54 @@
 BIG = 262144.0
 LOW = -1e30
 
-ORDER = ((0,), (8,), (16,), (1, 7), (9, 17), (2, 15), (6, 18), (10, 14), (3, 5))
-LAST = (4, 11, 12, 13)
+ORDER = ((0,), (8,), (16,), (1, 7), (6, 9), (15, 17), (2, 5), (10, 14), (13, 18))
+LAST = (3, 4, 11, 12)
 TICKS = (
     (
-        (1, 1, 1, 0, 1), (1, 3, 0, 3, 0), (1, 1, 0, 0, 1), (1, 2, 1, 1, 0), (1, 2, 0, 1, 0), (1, 0, 1, 0, 7),
-        (1, 0, 0, 0, 7),
-    ),
-    (
-        (0, 0, 3, 0), (1, 3, 0, 2, 0), (0, 1, 0, 1), (0, 1, 1, 0), (0, 1, 0, 7), (1, 1, 1, 0, 2),
-        (1, 1, 1, 1, 1), (1, 0, 1, 1, 7), (1, 0, 1, 0, 6), (1, 2, 1, 2, 0), (0, 0, 0, 1), (0, 0, 1, 0),
-        (0, 0, 0, 7), (1, 3, 0, 3, 7), (1, 2, 0, 1, 1), (1, 1, 0, 0, 2), (1, 3, 0, 3, 1), (1, 0, 0, 0, 6),
-        (1, 2, 0, 1, 7),
-    ),
-    (
-        (0, 0, 2, 0), (0, 0, 3, 7), (0, 1, 0, 2), (0, 1, 1, 7), (0, 1, 2, 0), (1, 2, 1, 2, 7),
-        (1, 3, 0, 2, 7), (1, 0, 1, 1, 6), (1, 1, 1, 0, 3),
-    ),
-    (
-        (0, 0, 3, 1), (0, 0, 1, 1), (1, 3, 0, 2, 1), (0, 1, 1, 1), (0, 1, 0, 6), (0, 0, 1, 7),
-        (1, 2, 1, 2, 1), (1, 1, 1, 1, 2), (1, 0, 1, 0, 5),
-    ),
-    (
-        (0, 0, 2, 7), (0, 0, 0, 2), (0, 0, 0, 6), (0, 0, 2, 1), (0, 1, 2, 7), (1, 1, 0, 0, 3),
-        (1, 0, 1, 2, 6), (1, 2, 0, 1, 6), (1, 2, 0, 1, 2), (1, 1, 0, 2, 2), (1, 0, 0, 0, 5), (1, 3, 0, 3, 6),
-        (3,),
-    ),
-    (
-        (0, 1, 1, 6), (0, 1, 0, 3), (0, 1, 2, 1), (0, 0, 3, 6), (0, 1, 1, 2), (0, 1, 0, 5), (2,),
-        (0, 0, 1, 6), (1, 1, 1, 2, 2), (1, 2, 1, 1, 3), (1, 3, 0, 2, 6), (1, 2, 1, 1, 5), (1, 1, 1, 0, 4),
-    ),
-    (
-        (0, 0, 0, 3), (0, 0, 1, 2), (0, 1, 2, 6), (0, 0, 2, 2), (0, 0, 2, 6), (1, 2, 0, 1, 3),
-        (1, 1, 0, 0, 4), (1, 1, 0, 2, 3), (1, 0, 1, 2, 5),
-    ),
-    (
-        (0, 0, 0, 5), (0, 1, 1, 3), (0, 1, 2, 2), (0, 1, 1, 5), (1, 0, 1, 1, 4), (1, 2, 0, 1, 5),
-        (1, 3, 0, 3, 5), (1, 2, 1, 2, 3),
-    ),
-    (
-        (0, 1, 2, 5), (0, 1, 0, 4), (0, 0, 1, 3), (0, 0, 0, 4), (0, 0, 1, 5), (0, 0, 3, 5), (0, 0, 2, 3),
-        (1, 0, 1, 2, 4), (1, 3, 0, 2, 5), (1, 1, 0, 2, 4), (1, 2, 0, 1, 4),
-    ),
-    (
-        (0, 1, 1, 4), (0, 1, 2, 3), (0, 0, 2, 5), (0, 0, 2, 4), (0, 0, 1, 4), (0, 1, 2, 4),
+        (1, 1, 0, 0, 1, 255), (1, 0, 0, 0, 7, 255), (1, 1, 1, 0, 1, 255), (1, 2, 1, 1, 0, 255),
+        (1, 3, 0, 3, 0, 255), (1, 2, 0, 1, 0, 255), (1, 0, 1, 0, 7, 255),
+    ),
+    (
+        (0, 0, 0, 1, 255), (1, 1, 0, 0, 2, 255), (1, 2, 0, 1, 1, 255), (0, 0, 0, 7, 255),
+        (1, 3, 0, 3, 7, 255), (1, 0, 0, 0, 6, 255), (0, 1, 0, 1, 255), (1, 1, 1, 0, 2, 255),
+        (0, 1, 1, 0, 255), (1, 2, 1, 2, 0, 255), (1, 1, 1, 1, 1, 255), (1, 0, 1, 1, 7, 255),
+        (0, 0, 0, 2, 255), (1, 1, 0, 0, 3, 255), (1, 2, 0, 1, 2, 255), (0, 0, 3, 0, 255),
+        (1, 3, 0, 2, 0, 255), (0, 0, 3, 7, 255), (1, 3, 0, 2, 7, 255), (0, 0, 1, 0, 255),
+        (1, 0, 0, 1, 7, 255),
+    ),
+    (
+        (0, 0, 0, 6, 255), (1, 3, 0, 3, 6, 255), (1, 0, 0, 0, 5, 255), (1, 2, 0, 1, 6, 255),
+        (0, 1, 0, 2, 255), (1, 2, 1, 1, 2, 255), (1, 1, 1, 0, 3, 195), (0, 0, 1, 1, 255),
+        (1, 2, 0, 2, 1, 127), (0, 1, 2, 0, 255), (1, 0, 1, 2, 7, 255), (1, 1, 1, 2, 1, 254),
+        (0, 0, 2, 0, 255),
+    ),
+    (
+        (0, 0, 3, 6, 255), (1, 3, 0, 2, 6, 255), (0, 1, 1, 1, 255), (0, 1, 1, 7, 255), (1, 0, 1, 1, 6, 255),
+        (0, 0, 0, 5, 255), (1, 2, 0, 1, 5, 255), (0, 1, 0, 7, 255), (1, 3, 1, 3, 7, 1), (1, 0, 1, 0, 6, 255),
+        (0, 0, 1, 7, 255),
+    ),
+    (
+        (0, 0, 0, 3, 255), (1, 2, 0, 1, 3, 255), (1, 1, 0, 0, 4, 225), (0, 1, 1, 2, 255),
+        (1, 1, 1, 1, 3, 255), (0, 1, 2, 7, 255), (0, 0, 1, 2, 255), (1, 2, 0, 2, 2, 63), (0, 0, 2, 7, 255),
+    ),
+    (
+        (0, 1, 3, 7, 1), (0, 0, 1, 5, 255), (1, 0, 0, 1, 4, 255), (1, 2, 0, 2, 5, 135), (0, 1, 1, 6, 255),
+        (1, 0, 1, 1, 5, 255), (1, 2, 1, 2, 6, 255), (0, 0, 1, 3, 255), (1, 2, 0, 2, 3, 31), (0, 1, 2, 1, 127),
+        (1, 1, 1, 2, 2, 126), (0, 0, 2, 1, 127),
+    ),
+    (
+        (0, 1, 1, 3, 255), (1, 1, 1, 1, 4, 255), (1, 2, 1, 2, 3, 31), (0, 0, 1, 4, 255), (0, 1, 0, 3, 225),
+        (1, 1, 1, 0, 4, 225), (0, 1, 0, 6, 255), (1, 0, 1, 0, 5, 124), (1, 3, 1, 3, 6, 3), (0, 0, 1, 6, 255),
+    ),
+    (
+        (0, 0, 2, 6, 255), (0, 0, 2, 5, 135), (1, 0, 0, 2, 4, 135), (0, 0, 0, 4, 240), (0, 0, 2, 2, 63),
+        (0, 0, 2, 3, 31), (0, 1, 1, 5, 255), (1, 2, 1, 2, 5, 7), (0, 1, 2, 2, 63), (0, 1, 2, 6, 255),
+    ),
+    (
+        (0, 1, 0, 5, 248), (0, 1, 3, 6, 3), (0, 1, 1, 4, 255), (0, 1, 2, 3, 31), (1, 1, 1, 2, 4, 30),
+    ),
+    (
+        (0, 1, 0, 4, 240), (0, 0, 2, 4, 15), (0, 1, 2, 5, 7), (0, 1, 2, 4, 15),
     ),
 )
 MESSAGES = tuple(item[1:] for tick in TICKS for item in tick if item[0] == 1)
@@ -82,7 +86,7 @@
 def kernel(
     q_ref, k_ref, v_ref, len_ref, w_ref, out_ref,
     qt, kv, acc, top, qpos, firsts, lasts, wts, att, far, near_r, near_l, mid_l, mid_r, in_l, in_r, mine,
-    kv_send, kv_recv, sp_send, sp_recv, w_local, w_send, w_recv, a_send, a_recv, x_send, x_recv,
+    kv_send, kv_recv, w_local, w_send, w_recv, a_send, a_recv, x_send, x_recv,
 ):
     ctx, tp = lax.axis_index("ctx"), lax.axis_index("tp")
     y, z = ctx // NZ, lax.rem(ctx, NZ)
@@ -97,7 +101,6 @@
     links = (z_next, z_back, y_next, y_back)
     shift = ((0, 1), (0, -1), (-1, 0), (1, 0))
 
-    kv[3, 6:8, 1:3] = jnp.zeros((2, 2, 2 * HEAD, HEAD), jnp.bfloat16)
     barrier = pltpu.get_barrier_semaphore()
     for device in links + (x_next, x_back, other):
         pl.semaphore_signal(barrier, inc=1, device_id=device, device_id_type=MESH)
@@ -133,34 +136,25 @@
             device_id_type=MESH,
         )
 
-    def special(at):
-        return pltpu.make_async_remote_copy(
-            src_ref=kv.at[0, 6 + at, pl.ds(1, 2)],
-            dst_ref=kv.at[3, 6 + at, pl.ds(1, 2)],
-            send_sem=sp_send.at[at],
-            recv_sem=sp_recv.at[at],
-            device_id=y_back,
-            device_id_type=MESH,
-        )
-
-    sends_special = (y == 0) & (z < 2)
-    takes_special = (y == NY - 1) & (z < 2)
+    def where(mask, run):
+        if mask == (1 << NZ) - 1:
+            run()
+            return
+        within = None
+        for first in range(NZ):
+            if mask >> first & 1 and not (first and mask >> (first - 1) & 1):
+                last = first
+                while mask >> (last + 1) & 1:
+                    last += 1
+                here = (z >= first) & (z <= last)
+                within = here if within is None else within | here
+        pl.when(within)(run)
 
     def act(item):
         if item[0] == 0:
-            arrival(*item[1:]).wait_recv()
-        elif item[0] == 1:
-            message(*item[1:]).start()
-        elif item[0] == 2:
-            @pl.when(sends_special)
-            def _():
-                for at in range(2):
-                    special(at).start()
+            where(item[-1], lambda: arrival(*item[1:-1]).wait_recv())
         else:
-            @pl.when(takes_special)
-            def _():
-                for at in range(2):
-                    special(at).wait_recv()
+            where(item[-1], lambda: message(*item[1:-1]).start())
 
     pl.semaphore_wait(barrier, 7)
     for item in TICKS[0]:
@@ -374,12 +368,7 @@
         for copy in copies(t):
             copy.wait_send()
     for item in MESSAGES:
-        message(*item).wait_send()
-
-    @pl.when(sends_special)
-    def _():
-        for at in range(2):
-            special(at).wait_send()
+        where(item[-1], lambda item=item: message(*item[:-1]).wait_send())
 
 
 def local(queries, keys, values, doc_lengths, out_weight):
@@ -411,8 +400,6 @@
             pltpu.VMEM((TILES, TILE, WIDE), f32),
             dma((2, NY, NZ)),
             dma((2, NY, NZ)),
-            dma((2,)),
-            dma((2,)),
             dma((NX,)),
             dma((NX,)),
             dma((NX,)),

time: 81.9 us -> 73.7 us (0.90)
  Pallas kernels: 79.9 us -> 71.2 us
    pallas_call x1, Pallas kernels: 79.9 us -> 71.2 us  [local(): pl.pallas_call(kernel, out_shape=jax.ShapeDtypeStruct((ROWS, WIDE), bf16)...]
where the time goes in v3:
time: 73.7 us; the launch traced here: 73 us
  Pallas kernels  71.2 us (97%)
  local copies, waits for them, and re-layouts  1.85 us (3%)
    pallas_call x1, Pallas kernels, local(): pl.pallas_call(kernel, out_shape=jax.ShapeDtypeStruct((ROWS, WIDE), bf16)...  71.2 us
    unnamed x1, local copies, waits for them, and re-layouts  1.85 us

profile of v3, /device:TPU:16, one launch (start us, length us, event | category | flops | bytes accessed | tf_op | source)
XLA Modules:
  0.0 73.0 jit_solution(12371927108339367765)
XLA Ops:
  0.0 71.2 %shard_map.55 = bf16[384,640]{1,0:T(8,128)(2,1)} custom-call(bf16[384,1024]{1,0:T(8,128)(2,1)} %q_ref.1, bf16[384,128]{1,0:T(8,128)(2,1)} %k_ref.1, bf16[384,128]{1,0:T(8,128)(2,1)} %v_ref.1, s32[24]{0:T(128)} %len_ref.1, bf16[1024,5120]{1,0:T(8,128)(2,1)} %w_ref.1), custom_call_target="tpu_custom_call" | custom-call | tf_op jit(solution)/shard_map/pallas_call | solution.py:378
  71.2 1.9 %copy.7 = bf16[384,640]{1,0:T(8,128)(2,1)} copy(bf16[384,640]{1,0:T(8,128)(2,1)} %shard_map.55) | data formatting | bytes 983040

commit v4 on v3

--- a/solution.py
+++ b/solution.py
@@ -23,54 +23,53 @@
 BIG = 262144.0
 LOW = -1e30
 
-ORDER = ((0,), (8,), (16,), (1, 7), (6, 9), (15, 17), (2, 5), (10, 14), (13, 18))
-LAST = (3, 4, 11, 12)
+SIZES = (2, 4, 4, 4, 4)
+ORDER = (
+    (7, 8, 1, 17, 18, 6, 5, 15, 2, 16, 9, 4, 3, 13, 14, 11, 10, 12),
+    (1, 7, 8, 9, 18, 6, 5, 15, 2, 16, 17, 4, 3, 13, 14, 11, 10, 12),
+    (1, 2, 7, 8, 9, 6, 5, 15, 10, 16, 17, 4, 3, 13, 14, 11, 18, 12),
+    (1, 2, 7, 8, 9, 3, 6, 5, 15, 10, 16, 17, 4, 11, 13, 14, 18, 12),
+    (1, 2, 7, 8, 9, 3, 6, 5, 15, 10, 16, 17, 12, 4, 11, 13, 14, 18),
+    (1, 2, 7, 8, 9, 3, 6, 13, 15, 10, 16, 17, 12, 4, 11, 14, 18, 5),
+    (1, 2, 7, 8, 9, 3, 14, 13, 6, 15, 10, 16, 17, 12, 4, 11, 18, 5),
+    (1, 2, 15, 7, 8, 9, 3, 14, 13, 6, 10, 16, 17, 12, 4, 11, 18, 5),
+)
 TICKS = (
     (
-        (1, 1, 0, 0, 1, 255), (1, 0, 0, 0, 7, 255), (1, 1, 1, 0, 1, 255), (1, 2, 1, 1, 0, 255),
-        (1, 3, 0, 3, 0, 255), (1, 2, 0, 1, 0, 255), (1, 0, 1, 0, 7, 255),
-    ),
-    (
-        (0, 0, 0, 1, 255), (1, 1, 0, 0, 2, 255), (1, 2, 0, 1, 1, 255), (0, 0, 0, 7, 255),
-        (1, 3, 0, 3, 7, 255), (1, 0, 0, 0, 6, 255), (0, 1, 0, 1, 255), (1, 1, 1, 0, 2, 255),
-        (0, 1, 1, 0, 255), (1, 2, 1, 2, 0, 255), (1, 1, 1, 1, 1, 255), (1, 0, 1, 1, 7, 255),
-        (0, 0, 0, 2, 255), (1, 1, 0, 0, 3, 255), (1, 2, 0, 1, 2, 255), (0, 0, 3, 0, 255),
-        (1, 3, 0, 2, 0, 255), (0, 0, 3, 7, 255), (1, 3, 0, 2, 7, 255), (0, 0, 1, 0, 255),
-        (1, 0, 0, 1, 7, 255),
-    ),
-    (
-        (0, 0, 0, 6, 255), (1, 3, 0, 3, 6, 255), (1, 0, 0, 0, 5, 255), (1, 2, 0, 1, 6, 255),
-        (0, 1, 0, 2, 255), (1, 2, 1, 1, 2, 255), (1, 1, 1, 0, 3, 195), (0, 0, 1, 1, 255),
-        (1, 2, 0, 2, 1, 127), (0, 1, 2, 0, 255), (1, 0, 1, 2, 7, 255), (1, 1, 1, 2, 1, 254),
-        (0, 0, 2, 0, 255),
-    ),
-    (
-        (0, 0, 3, 6, 255), (1, 3, 0, 2, 6, 255), (0, 1, 1, 1, 255), (0, 1, 1, 7, 255), (1, 0, 1, 1, 6, 255),
-        (0, 0, 0, 5, 255), (1, 2, 0, 1, 5, 255), (0, 1, 0, 7, 255), (1, 3, 1, 3, 7, 1), (1, 0, 1, 0, 6, 255),
-        (0, 0, 1, 7, 255),
-    ),
-    (
-        (0, 0, 0, 3, 255), (1, 2, 0, 1, 3, 255), (1, 1, 0, 0, 4, 225), (0, 1, 1, 2, 255),
-        (1, 1, 1, 1, 3, 255), (0, 1, 2, 7, 255), (0, 0, 1, 2, 255), (1, 2, 0, 2, 2, 63), (0, 0, 2, 7, 255),
-    ),
-    (
-        (0, 1, 3, 7, 1), (0, 0, 1, 5, 255), (1, 0, 0, 1, 4, 255), (1, 2, 0, 2, 5, 135), (0, 1, 1, 6, 255),
-        (1, 0, 1, 1, 5, 255), (1, 2, 1, 2, 6, 255), (0, 0, 1, 3, 255), (1, 2, 0, 2, 3, 31), (0, 1, 2, 1, 127),
-        (1, 1, 1, 2, 2, 126), (0, 0, 2, 1, 127),
-    ),
-    (
-        (0, 1, 1, 3, 255), (1, 1, 1, 1, 4, 255), (1, 2, 1, 2, 3, 31), (0, 0, 1, 4, 255), (0, 1, 0, 3, 225),
-        (1, 1, 1, 0, 4, 225), (0, 1, 0, 6, 255), (1, 0, 1, 0, 5, 124), (1, 3, 1, 3, 6, 3), (0, 0, 1, 6, 255),
-    ),
-    (
-        (0, 0, 2, 6, 255), (0, 0, 2, 5, 135), (1, 0, 0, 2, 4, 135), (0, 0, 0, 4, 240), (0, 0, 2, 2, 63),
-        (0, 0, 2, 3, 31), (0, 1, 1, 5, 255), (1, 2, 1, 2, 5, 7), (0, 1, 2, 2, 63), (0, 1, 2, 6, 255),
-    ),
-    (
-        (0, 1, 0, 5, 248), (0, 1, 3, 6, 3), (0, 1, 1, 4, 255), (0, 1, 2, 3, 31), (1, 1, 1, 2, 4, 30),
-    ),
-    (
-        (0, 1, 0, 4, 240), (0, 0, 2, 4, 15), (0, 1, 2, 5, 7), (0, 1, 2, 4, 15),
+        (1, 0, 0, 0, 7, 255), (1, 2, 0, 1, 0, 255), (1, 3, 0, 3, 0, 255), (1, 1, 1, 0, 1, 255),
+        (1, 0, 1, 0, 7, 255), (1, 2, 1, 1, 0, 255), (1, 1, 0, 0, 1, 3),
+    ),
+    (
+        (0, 0, 0, 7, 255), (1, 0, 0, 0, 6, 255), (1, 2, 0, 1, 7, 255), (1, 3, 0, 3, 7, 255),
+        (0, 0, 1, 0, 255), (1, 1, 0, 1, 1, 255), (0, 0, 3, 0, 255), (1, 3, 0, 2, 0, 255), (0, 1, 0, 1, 255),
+        (1, 2, 1, 1, 1, 255), (1, 1, 1, 0, 2, 129), (0, 1, 0, 7, 255), (1, 0, 1, 0, 6, 255),
+        (1, 2, 1, 1, 7, 255), (1, 3, 1, 3, 7, 1), (0, 0, 0, 6, 255), (1, 0, 0, 0, 5, 255),
+        (1, 3, 0, 3, 6, 255), (0, 0, 1, 1, 255), (1, 1, 0, 1, 2, 255), (0, 0, 2, 0, 255),
+        (1, 1, 0, 2, 1, 254), (0, 1, 0, 6, 255), (1, 0, 1, 0, 5, 255), (1, 3, 1, 3, 6, 3), (0, 1, 1, 0, 255),
+        (1, 2, 1, 2, 0, 255), (0, 1, 1, 1, 255), (1, 1, 1, 1, 2, 255), (1, 2, 1, 2, 1, 127),
+        (0, 0, 0, 5, 255), (1, 0, 0, 0, 4, 120), (1, 3, 0, 3, 5, 135), (1, 2, 0, 1, 5, 255),
+        (0, 0, 1, 2, 255), (1, 1, 0, 1, 3, 255), (0, 0, 1, 7, 255), (1, 0, 0, 1, 6, 255), (0, 0, 2, 1, 127),
+        (1, 1, 0, 2, 2, 126), (0, 0, 3, 7, 255), (1, 3, 0, 2, 7, 255),
+    ),
+    (
+        (0, 0, 0, 1, 129), (1, 1, 0, 0, 2, 129), (0, 0, 3, 6, 255), (1, 3, 0, 2, 6, 255), (0, 1, 1, 7, 255),
+        (1, 0, 1, 1, 6, 255), (0, 1, 0, 5, 255), (1, 0, 1, 0, 4, 120), (1, 2, 1, 1, 5, 255),
+        (0, 1, 1, 2, 255), (1, 1, 1, 1, 3, 255), (0, 1, 3, 6, 3), (0, 1, 3, 7, 1),
+    ),
+    (
+        (0, 0, 0, 4, 240), (1, 0, 0, 0, 3, 112), (0, 0, 3, 5, 135), (1, 3, 0, 2, 5, 135), (0, 0, 2, 2, 63),
+        (0, 0, 0, 2, 192), (0, 0, 1, 3, 255), (1, 1, 0, 1, 4, 255), (1, 2, 0, 2, 3, 31), (0, 1, 0, 2, 192),
+        (0, 1, 1, 3, 255), (1, 2, 1, 2, 3, 31), (1, 1, 1, 1, 4, 255), (0, 1, 1, 6, 255), (1, 2, 1, 2, 6, 255),
+        (0, 1, 2, 0, 255), (1, 0, 1, 2, 7, 255), (0, 1, 2, 1, 127), (1, 1, 1, 2, 2, 126), (0, 0, 1, 6, 255),
+    ),
+    (
+        (0, 0, 2, 5, 135), (1, 0, 0, 2, 4, 135), (0, 1, 2, 3, 31), (1, 1, 1, 2, 4, 30), (0, 0, 1, 5, 255),
+        (0, 1, 0, 4, 240), (1, 0, 1, 0, 3, 112), (0, 1, 1, 4, 255), (0, 1, 1, 5, 255), (1, 2, 1, 2, 5, 7),
+        (0, 1, 2, 7, 255), (0, 0, 1, 4, 255), (0, 0, 2, 3, 31), (0, 0, 2, 7, 255),
+    ),
+    (
+        (0, 1, 2, 4, 15), (0, 1, 2, 6, 255), (0, 1, 0, 3, 224), (0, 1, 2, 2, 63), (0, 1, 2, 5, 7),
+        (0, 0, 0, 3, 224), (0, 0, 2, 4, 15), (0, 0, 2, 6, 255),
     ),
 )
 MESSAGES = tuple(item[1:] for tick in TICKS for item in tick if item[0] == 1)
@@ -85,8 +84,8 @@
 
 def kernel(
     q_ref, k_ref, v_ref, len_ref, w_ref, out_ref,
-    qt, kv, acc, top, qpos, firsts, lasts, wts, att, far, near_r, near_l, mid_l, mid_r, in_l, in_r, mine,
-    kv_send, kv_recv, w_local, w_send, w_recv, a_send, a_recv, x_send, x_recv,
+    q_own, qt, kv, acc, top, qpos, firsts, lasts, wts, att, far, near_r, near_l, mid_l, mid_r, in_l, in_r, mine,
+    q_sem, kv_send, kv_recv, w_local, w_send, w_recv, a_send, a_recv, x_send, x_recv,
 ):
     ctx, tp = lax.axis_index("ctx"), lax.axis_index("tp")
     y, z = ctx // NZ, lax.rem(ctx, NZ)
@@ -101,6 +100,8 @@
     links = (z_next, z_back, y_next, y_back)
     shift = ((0, 1), (0, -1), (-1, 0), (1, 0))
 
+    q_copy = pltpu.make_async_copy(q_ref, q_own, q_sem)
+    q_copy.start()
     barrier = pltpu.get_barrier_semaphore()
     for device in links + (x_next, x_back, other):
         pl.semaphore_signal(barrier, inc=1, device_id=device, device_id_type=MESH)
@@ -163,15 +164,19 @@
     def weight_columns(xx, half):
         return pl.ds(pl.multiple_of(xx * (2 * WIDE) + half * WIDE, HEAD), WIDE)
 
-    def weight_keep(xx):
-        return pltpu.make_async_copy(w_ref.at[:, weight_columns(xx, core)], wts.at[core, xx], w_local.at[xx])
-
-    def weight_give(xx):
+    targets = [lax.rem(x + ahead, NX) for ahead in (2, 1, 3, 0)]
+
+    def weight_keep(at):
+        return pltpu.make_async_copy(
+            w_ref.at[:, weight_columns(targets[at], core)], wts.at[core, :, pl.ds(at * WIDE, WIDE)], w_local.at[at]
+        )
+
+    def weight_give(at):
         return pltpu.make_async_remote_copy(
-            src_ref=w_ref.at[:, weight_columns(xx, 1 - core)],
-            dst_ref=wts.at[core, xx],
-            send_sem=w_send.at[xx],
-            recv_sem=w_recv.at[xx],
+            src_ref=w_ref.at[:, weight_columns(targets[at], 1 - core)],
+            dst_ref=wts.at[core, :, pl.ds(at * WIDE, WIDE)],
+            send_sem=w_send.at[at],
+            recv_sem=w_recv.at[at],
             device_id=other,
             device_id_type=MESH,
         )
@@ -195,8 +200,9 @@
     lasts[...] = last_l
     own = ctx * ROWS + lax.broadcasted_iota(jnp.int32, (HEAD, ROWS), 1)
     apart = jnp.where((own >= first_s) & (own < last_s), 0.0, -BIG).astype(jnp.bfloat16)
+    q_copy.wait()
     for h in range(GROUP):
-        turned = q_ref[:, h * HEAD:(h + 1) * HEAD].astype(jnp.float32).T.astype(jnp.bfloat16)
+        turned = q_own[:, h * HEAD:(h + 1) * HEAD].astype(jnp.float32).T.astype(jnp.bfloat16)
         for t in range(TILES):
             span = slice(t * SPAN + h * TILE, t * SPAN + (h + 1) * TILE)
             rows = slice(t * TILE, (t + 1) * TILE)
@@ -256,28 +262,43 @@
             got, held = ahead, soft
         gather(steps - 1, *held)
 
+    order = [pick(z, [row[at] for row in ORDER]) for at in range(len(ORDER[0]))]
+    groups, at = [[jnp.int32(0)]], 0
+    for size in SIZES:
+        groups.append(order[at:at + size])
+        at += size
+    last = groups.pop()
+    sizes = [len(group) for group in groups]
+
+    def least(deltas):
+        return functools.reduce(jnp.minimum, deltas)
+
     def step(i, carry):
-        for at in range(1, len(ORDER)):
+        for at in range(1, len(groups)):
             @pl.when(i == at)
             def _(at=at):
                 for item in TICKS[at]:
                     act(item)
-        one = pick(i, [min(group) for group in ORDER])
-        two = pick(i, [max(group) for group in ORDER])
-
-        @pl.when((one == two) & (ctx >= one))
-        def _():
-            attend((one,), True, 0, COLS // CHUNK)
-
-        @pl.when((one != two) & (ctx >= one))
-        def _():
-            attend((one, two), False, 0, COLS // CHUNK)
+
+        for size in sorted(set(sizes)):
+            deltas = []
+            for slot in range(size):
+                value = groups[0][0]
+                for at, group in enumerate(groups):
+                    if len(group) == size:
+                        value = jnp.where(i == at, group[slot], value)
+                deltas.append(value)
+            now = functools.reduce(jnp.logical_or, [i == at for at in range(len(groups)) if sizes[at] == size])
+
+            @pl.when(now & (ctx >= least(deltas)))
+            def _(deltas=tuple(deltas), size=size):
+                attend(deltas, size == 1, 0, COLS // CHUNK)
 
         return carry
 
-    lax.fori_loop(0, len(ORDER), step, 0)
-
-    for item in TICKS[len(ORDER)]:
+    lax.fori_loop(0, len(groups), step, 0)
+
+    for item in TICKS[len(groups)]:
         act(item)
     for xx in range(NX):
         weight_keep(xx).wait()
@@ -325,13 +346,13 @@
     def finish(t, carry):
         base = t * SPAN
 
-        @pl.when(ctx >= min(LAST))
+        @pl.when(ctx >= least(last))
         def _():
-            attend(LAST, False, base, SPAN // CHUNK)
+            attend(tuple(last), False, base, SPAN // CHUNK)
 
         for h in range(GROUP):
             span = pl.ds(pl.multiple_of(base + h * TILE, TILE), TILE)
-            rows = acc[0:HEAD, span] / acc[HEAD:HEAD + 1, span]
+            rows = acc[0:HEAD, span] * (1.0 / acc[HEAD:HEAD + 1, span])
             att[core, t, :, h * HEAD:(h + 1) * HEAD] = rows.T.astype(jnp.bfloat16)
         swap(t).start()
 
@@ -339,22 +360,22 @@
         def _():
             pass_on(t - 1)
 
-        targets = [lax.rem(x + step, NX) for step in (2, 1, 3, 0)]
-        sums = [jnp.dot(att[core, t], wts[core, xx], preferred_element_type=jnp.float32) for xx in targets]
+        def term(of, at):
+            return jnp.dot(att[of, t], wts[of, :, 2 * at * WIDE:2 * (at + 1) * WIDE], preferred_element_type=jnp.float32)
+
+        far_up, far_down, up, down, _, _ = copies(t)
+        total = term(core, 0)
         swap(t).wait()
-
-        def whole(at):
-            return sums[at] + jnp.dot(att[1 - core, t], wts[1 - core, targets[at]], preferred_element_type=jnp.float32)
-
-        far_up, far_down, up, down, _, _ = copies(t)
-        far[t] = whole(0).astype(jnp.bfloat16)
+        total += term(1 - core, 0)
+        far[t] = total[:, 0:WIDE].astype(jnp.bfloat16)
         far_up.start()
         far_down.start()
-        near_r[t] = whole(1).astype(jnp.bfloat16)
+        near_r[t] = total[:, WIDE:].astype(jnp.bfloat16)
         up.start()
-        near_l[t] = whole(2).astype(jnp.bfloat16)
+        total = term(core, 1) + term(1 - core, 1)
+        near_l[t] = total[:, 0:WIDE].astype(jnp.bfloat16)
         down.start()
-        mine[t] = whole(3)
+        mine[t] = total[:, WIDE:]
         return carry
 
     lax.fori_loop(0, TILES, finish, 0)
@@ -378,9 +399,10 @@
     return pl.pallas_call(
         kernel,
         out_shape=jax.ShapeDtypeStruct((ROWS, WIDE), bf16),
-        in_specs=[vmem, vmem, vmem, pl.BlockSpec(memory_space=pltpu.SMEM), pl.BlockSpec(memory_space=pl.ANY)],
+        in_specs=[pl.BlockSpec(memory_space=pl.ANY), vmem, vmem, pl.BlockSpec(memory_space=pltpu.SMEM), pl.BlockSpec(memory_space=pl.ANY)],
         out_specs=vmem,
         scratch_shapes=[
+            pltpu.VMEM((ROWS, GROUP * HEAD), bf16),
             pltpu.VMEM((2 * HEAD, COLS), bf16),
             pltpu.VMEM((NY, NZ, 3, 2 * HEAD, HEAD), bf16),
             pltpu.VMEM((HEAD + 16, COLS), f32),
@@ -388,7 +410,7 @@
             pltpu.VMEM((8, COLS), jnp.int32),
             pltpu.VMEM((8, HEAD), jnp.int32),
             pltpu.VMEM((8, HEAD), jnp.int32),
-            pltpu.VMEM((NK, NX, GROUP * HEAD, WIDE), bf16),
+            pltpu.VMEM((NK, GROUP * HEAD, NX * WIDE), bf16),
             pltpu.VMEM((NK, TILES, TILE, GROUP * HEAD), bf16),
             pltpu.VMEM((TILES, TILE, WIDE), bf16),
             pltpu.VMEM((TILES, TILE, WIDE), bf16),
@@ -398,6 +420,7 @@
             pltpu.VMEM((TILES, TILE, WIDE), bf16),
             pltpu.VMEM((TILES, TILE, WIDE), bf16),
             pltpu.VMEM((TILES, TILE, WIDE), f32),
+            dma,
             dma((2, NY, NZ)),
             dma((2, NY, NZ)),
             dma((NX,)),

time: 73.7 us -> 71.6 us (0.972)
  Pallas kernels: 71.2 us -> 69.6 us
    pallas_call x1, Pallas kernels: 71.2 us -> 69.6 us  [local(): pl.pallas_call(kernel, out_shape=jax.ShapeDtypeStruct((ROWS, WIDE), bf16)...]
where the time goes in v4:
time: 71.6 us; the launch traced here: 71.4 us
  Pallas kernels  69.6 us (97%)
  local copies, waits for them, and re-layouts  1.85 us (3%)
    pallas_call x1, Pallas kernels, local(): pl.pallas_call(kernel, out_shape=jax.ShapeDtypeStruct((ROWS, WIDE), bf16)...  69.6 us
    unnamed x1, local copies, waits for them, and re-layouts  1.85 us

profile of v4, /device:TPU:16, one launch (start us, length us, event | category | flops | bytes accessed | tf_op | source)
XLA Modules:
  0.0 71.4 jit_solution(6850707707405129624)
XLA Ops:
  0.0 69.6 %shard_map.55 = bf16[384,640]{1,0:T(8,128)(2,1)} custom-call(bf16[384,1024]{1,0:T(8,128)(2,1)} %q_ref.1, bf16[384,128]{1,0:T(8,128)(2,1)} %k_ref.1, bf16[384,128]{1,0:T(8,128)(2,1)} %v_ref.1, s32[24]{0:T(128)} %len_ref.1, bf16[1024,5120]{1,0:T(8,128)(2,1)} %w_ref.1), custom_call_target="tpu_custom_call" | custom-call | tf_op jit(solution)/shard_map/pallas_call | solution.py:399
  69.6 1.9 %copy.7 = bf16[384,640]{1,0:T(8,128)(2,1)} copy(bf16[384,640]{1,0:T(8,128)(2,1)} %shard_map.55) | data formatting | bytes 983040

commit v5 on v4

--- a/solution.py
+++ b/solution.py
@@ -371,20 +371,26 @@
         far_up.start()
         far_down.start()
         near_r[t] = total[:, WIDE:].astype(jnp.bfloat16)
-        up.start()
         total = term(core, 1) + term(1 - core, 1)
         near_l[t] = total[:, 0:WIDE].astype(jnp.bfloat16)
+        up.start()
         down.start()
         mine[t] = total[:, WIDE:]
         return carry
 
     lax.fori_loop(0, TILES, finish, 0)
-    pass_on(TILES - 1)
-    for t in range(TILES):
+
+    def add_up(t):
         for copy in copies(t)[2:]:
             copy.wait_recv()
         total = mine[t] + in_l[t].astype(jnp.float32) + in_r[t].astype(jnp.float32)
         out_ref[t * TILE:(t + 1) * TILE] = total.astype(jnp.bfloat16)
+
+    for t in range(TILES - 2):
+        add_up(t)
+    pass_on(TILES - 1)
+    for t in range(TILES - 2, TILES):
+        add_up(t)
     for t in range(TILES):
         for copy in copies(t):
             copy.wait_send()

time: 71.6 us -> 71.4 us (level)
  no operation moved by 1% of the time
where the time goes in v5:
time: 71.4 us; the launch traced here: 71.2 us
  Pallas kernels  69.3 us (97%)
  local copies, waits for them, and re-layouts  1.85 us (3%)
    pallas_call x1, Pallas kernels, local(): pl.pallas_call(kernel, out_shape=jax.ShapeDtypeStruct((ROWS, WIDE), bf16)...  69.3 us
    unnamed x1, local copies, waits for them, and re-layouts  1.85 us

profile of v5, /device:TPU:16, one launch (start us, length us, event | category | flops | bytes accessed | tf_op | source)
XLA Modules:
  0.0 71.2 jit_solution(8746042854906731754)
XLA Ops:
  0.0 69.3 %shard_map.55 = bf16[384,640]{1,0:T(8,128)(2,1)} custom-call(bf16[384,1024]{1,0:T(8,128)(2,1)} %q_ref.1, bf16[384,128]{1,0:T(8,128)(2,1)} %k_ref.1, bf16[384,128]{1,0:T(8,128)(2,1)} %v_ref.1, s32[24]{0:T(128)} %len_ref.1, bf16[1024,5120]{1,0:T(8,128)(2,1)} %w_ref.1), custom_call_target="tpu_custom_call" | custom-call | tf_op jit(solution)/shard_map/pallas_call | solution.py:405
  69.3 1.9 %copy.7 = bf16[384,640]{1,0:T(8,128)(2,1)} copy(bf16[384,640]{1,0:T(8,128)(2,1)} %shard_map.55) | data formatting | bytes 983040

commit v6 on v5

--- a/solution.py
+++ b/solution.py
@@ -306,10 +306,10 @@
 
     half = TILE // 2
 
-    def swap(t):
-        held = att.at[core, t]
+    def swap(t, part):
+        held = att.at[core, t, :, pl.ds(part * GROUP * HEAD // 2, GROUP * HEAD // 2)]
         return pltpu.make_async_remote_copy(
-            src_ref=held, dst_ref=held, send_sem=a_send.at[t], recv_sem=a_recv.at[t], device_id=other, device_id_type=MESH,
+            src_ref=held, dst_ref=held, send_sem=a_send.at[t, part], recv_sem=a_recv.at[t, part], device_id=other, device_id_type=MESH,
         )
 
     def along(t, at, src, dst, device):
@@ -354,7 +354,8 @@
             span = pl.ds(pl.multiple_of(base + h * TILE, TILE), TILE)
             rows = acc[0:HEAD, span] * (1.0 / acc[HEAD:HEAD + 1, span])
             att[core, t, :, h * HEAD:(h + 1) * HEAD] = rows.T.astype(jnp.bfloat16)
-        swap(t).start()
+            if h % (GROUP // 2) == GROUP // 2 - 1:
+                swap(t, h // (GROUP // 2)).start()
 
         @pl.when(t > 0)
         def _():
@@ -365,7 +366,8 @@
 
         far_up, far_down, up, down, _, _ = copies(t)
         total = term(core, 0)
-        swap(t).wait()
+        for part in range(2):
+            swap(t, part).wait()
         total += term(1 - core, 0)
         far[t] = total[:, 0:WIDE].astype(jnp.bfloat16)
         far_up.start()
@@ -432,8 +434,8 @@
             dma((NX,)),
             dma((NX,)),
             dma((NX,)),
-            dma((TILES,)),
-            dma((TILES,)),
+            dma((TILES, 2)),
+            dma((TILES, 2)),
             dma((TILES, 6)),
             dma((TILES, 6)),
         ],

time: 71.4 us -> 71.3 us (level)
  no operation moved by 1% of the time
where the time goes in v6:
time: 71.3 us; the launch traced here: 71.1 us
  Pallas kernels  69.3 us (97%)
  local copies, waits for them, and re-layouts  1.85 us (3%)
    pallas_call x1, Pallas kernels, local(): pl.pallas_call(kernel, out_shape=jax.ShapeDtypeStruct((ROWS, WIDE), bf16)...  69.3 us
    unnamed x1, local copies, waits for them, and re-layouts  1.85 us

profile of v6, /device:TPU:16, one launch (start us, length us, event | category | flops | bytes accessed | tf_op | source)
XLA Modules:
  0.0 71.1 jit_solution(6814625583635677258)
XLA Ops:
  0.0 69.3 %shard_map.55 = bf16[384,640]{1,0:T(8,128)(2,1)} custom-call(bf16[384,1024]{1,0:T(8,128)(2,1)} %q_ref.1, bf16[384,128]{1,0:T(8,128)(2,1)} %k_ref.1, bf16[384,128]{1,0:T(8,128)(2,1)} %v_ref.1, s32[24]{0:T(128)} %len_ref.1, bf16[1024,5120]{1,0:T(8,128)(2,1)} %w_ref.1), custom_call_target="tpu_custom_call" | custom-call | tf_op jit(solution)/shard_map/pallas_call | solution.py:407
  69.3 1.9 %copy.7 = bf16[384,640]{1,0:T(8,128)(2,1)} copy(bf16[384,640]{1,0:T(8,128)(2,1)} %shard_map.55) | data formatting | bytes 983040
